TPU v7x, 32 devices: a whole 2x2x4 slice. The times are simulated.
32 devices in a mesh: member: 4 (over x, core), tile: 8 (over z, y).
Axes of the slice: x: 2, y: 2, z: 4, core: 2. Of those that a mesh axis runs over, the one named last changes fastest.
Arguments:
- upsampled_coarse: bfloat16 [32, 32, 256], P('tile'), may hold values from -6 to 6
- target: bfloat16 [32, 32, 256], P('tile'), may hold values from -6 to 6
- seeds: int32 [8], P('member'), may hold values from 0 to 63
- band_row: int32 [1], replicated, may hold values from 0 to 2016
- noise_bank: float32 [64, 16], replicated, may hold values from -5 to 5
- cond_weight: float32 [16, 256], replicated, may hold values from -1.5 to 1.5
- conv_in: bfloat16 [3, 3, 32, 128], replicated, may hold values from -0.375 to 0.375
- conv_mid: bfloat16 [3, 3, 128, 128], replicated, may hold values from -0.1875 to 0.1875
- conv_out: bfloat16 [3, 3, 128, 128], replicated, may hold values from -0.1875 to 0.1875
- head_weight: bfloat16 [128, 32], replicated, may hold values from -0.5 to 0.5
- per_quantity_offset: float32 [32], replicated, may hold values from -3 to 3
Outputs:
- crps_map: float32 [32, 32, 256], P('tile', 'member')
- conv_grad: float32 [3, 3, 128, 128], replicated
- head_grad: float32 [128, 32], replicated
- bias_grad: float32 [32], replicated
Inputs may be any that keep to these rules, and one draw needn't show every extreme that they name: `band_row`: the band lies inside the grid.
All inputs are finite; a program needn't handle non-finite values.
Results may differ from a plain program's by a relative error of at most 0.0015.
Values may be sent and summed in bfloat16 or wider, within the bound.
A program may use at most 64 MiB of HBM per device.

v0:
```python
import math

import jax
import jax.numpy as jnp
from jax import lax
from jax.sharding import PartitionSpec as P

GRID_ROWS = 2048


def extended(x, sides, width):
    for axis, dim in sides:
        devices, length = (lax.axis_size(axis), x.shape[dim])
        up = [(i, (i + 1) % devices) for i in range(devices - 1)]
        down = [(j, i) for i, j in up]
        last = lax.slice_in_dim(x, length - width, length, axis=dim)
        first = lax.slice_in_dim(x, 0, width, axis=dim)
        before = lax.ppermute(last, axis, up)
        after = lax.ppermute(first, axis, down)
        x = jnp.concatenate([before, x, after], axis=dim)
    return x


def input_conv(padded, kernel):
    out_rows = padded.shape[0] - 2
    col_count = padded.shape[2]
    wide = jnp.pad(padded, ((0, 0), (0, 0), (1, 1)))
    summed = jnp.zeros((out_rows, col_count, kernel.shape[3]), jnp.float32)
    for i in range(3):
        for j in range(3):
            summed = summed + jnp.einsum(
                "rkw,kc->rwc",
                wide[i : i + out_rows, :, j : j + col_count],
                kernel[i, j],
                preferred_element_type=jnp.float32,
            )
    return summed


def feature_conv(padded, kernel):
    out_rows = padded.shape[1] - 2
    col_count = padded.shape[2]
    wide = jnp.pad(padded, ((0, 0), (0, 0), (1, 1), (0, 0)))
    summed = jnp.zeros((padded.shape[0], out_rows, col_count, kernel.shape[3]), jnp.float32)
    for i in range(3):
        for j in range(3):
            summed = summed + jnp.einsum(
                "mrwc,cd->mrwd",
                wide[:, i : i + out_rows, j : j + col_count],
                kernel[i, j],
                preferred_element_type=jnp.float32,
            )
    return summed


def condition(base, cond_scale, cond_shift):
    average = jnp.mean(base, axis=-1, keepdims=True)
    centred = base - average
    spread = jnp.mean(centred * centred, axis=-1, keepdims=True)
    normed = centred * lax.rsqrt(spread + 1e-05)
    mixed = normed[None] * (1.0 + cond_scale[:, None, None, :]) + cond_shift[:, None, None, :]
    return jax.nn.gelu(mixed).astype(jnp.bfloat16)


def abs_terms(probe, sample_group_predictions):

    def abs_single(member_index):
        return jnp.sum(jnp.abs(member_index[None] - sample_group_predictions), axis=0)

    return lax.map(abs_single, probe)


def sign_terms(probe, sample_group_predictions):

    def sign_single(member_index):
        return jnp.sum(jnp.sign(member_index[None] - sample_group_predictions), axis=0)

    return lax.map(sign_single, probe)


def on_device(
    upsampled_coarse,
    target,
    seeds,
    band_row,
    noise_bank,
    cond_weight,
    conv_in,
    conv_mid,
    conv_out,
    head_weight,
    per_quantity_offset,
):
    channels = conv_mid.shape[3]
    row_count = upsampled_coarse.shape[0]
    var_count = upsampled_coarse.shape[1]
    col_count = upsampled_coarse.shape[2]
    tile_count = lax.axis_size("tile")
    tile_at = lax.axis_index("tile")
    band_rows = row_count * tile_count
    selector = (seeds[:, None] == jnp.arange(noise_bank.shape[0], dtype=jnp.int32)[None]).astype(
        jnp.float32
    )
    noise_vec = jnp.dot(selector, noise_bank, precision=lax.Precision.HIGHEST)
    random_latent_gain = jnp.dot(noise_vec, cond_weight, precision=lax.Precision.HIGHEST)
    cond_scale = random_latent_gain[:, :channels]
    cond_shift = random_latent_gain[:, channels:]
    input_padded = extended(upsampled_coarse, (("tile", 0),), 1)
    first_hidden = condition(input_conv(input_padded, conv_in), cond_scale, cond_shift)
    first_padded = extended(first_hidden, (("tile", 1),), 1)
    latent_layer_two = jax.nn.gelu(feature_conv(first_padded, conv_mid)).astype(jnp.bfloat16)
    second_padded = extended(latent_layer_two, (("tile", 1),), 1)
    final_linear_response = feature_conv(second_padded, conv_out)
    latent_layer_three = (
        first_hidden.astype(jnp.float32) + jax.nn.gelu(final_linear_response)
    ).astype(jnp.bfloat16)
    final_layer_result = jnp.einsum(
        "mrwc,cv->mrvw", latent_layer_three, head_weight, preferred_element_type=jnp.float32
    )
    sample_prediction = (
        final_layer_result
        + upsampled_coarse.astype(jnp.float32)[None]
        + per_quantity_offset[None, None, :, None]
    ).astype(jnp.bfloat16)
    row_global = band_row[0] + tile_at * row_count + jnp.arange(row_count, dtype=jnp.int32)
    latitude = math.pi * (row_global.astype(jnp.float32) + 0.5) / GRID_ROWS - math.pi / 2
    row_factor = (jnp.cos(latitude) / (band_rows * col_count))[None, :, None, None]
    var_share = var_count // lax.axis_size("member")
    var_start = lax.axis_index("member") * var_share
    collected_members = lax.all_to_all(
        sample_prediction, "member", split_axis=2, concat_axis=0, tiled=True
    )
    sample_group_predictions = collected_members.astype(jnp.float32)
    member_count = sample_group_predictions.shape[0]
    truth = lax.dynamic_slice_in_dim(target, var_start, var_share, 1).astype(jnp.float32)
    abs_sums = abs_terms(sample_group_predictions, sample_group_predictions)
    sign_sums = sign_terms(sample_group_predictions, sample_group_predictions)
    crps_map = jnp.mean(jnp.abs(sample_group_predictions - truth[None]), axis=0) - jnp.sum(
        abs_sums, axis=0
    ) / (2 * member_count * (member_count - 1))
    cot_share = (
        row_factor
        * (
            jnp.sign(sample_group_predictions - truth[None]) / member_count
            - sign_sums / (member_count * (member_count - 1))
        )
    ).astype(jnp.bfloat16)
    cotangent = lax.all_to_all(cot_share, "member", split_axis=0, concat_axis=2, tiled=True)
    head_grad = jnp.einsum(
        "mrwc,mrvw->cv", latent_layer_three, cotangent, preferred_element_type=jnp.float32
    )
    bias_grad = jnp.sum(cotangent.astype(jnp.float32), axis=(0, 1, 3))
    back = jnp.einsum("mrvw,cv->mrwc", cotangent, head_weight, preferred_element_type=jnp.float32)
    unused_out, pullback = jax.vjp(jax.nn.gelu, final_linear_response)
    d_pre = pullback(back)[0].astype(jnp.bfloat16)
    second_wide = jnp.pad(second_padded, ((0, 0), (0, 0), (1, 1), (0, 0)))
    rows_of = []
    for i in range(3):
        cols_of = []
        for j in range(3):
            cols_of.append(
                jnp.einsum(
                    "mrwc,mrwd->cd",
                    second_wide[:, i : i + row_count, j : j + col_count],
                    d_pre,
                    preferred_element_type=jnp.float32,
                )
            )
        rows_of.append(jnp.stack(cols_of))
    conv_grad = jnp.stack(rows_of)
    conv_grad, head_grad, bias_grad = lax.psum(
        (conv_grad, head_grad, bias_grad), ("member", "tile")
    )
    return (crps_map, conv_grad, head_grad, bias_grad)


def solution(mesh):
    return jax.shard_map(
        on_device,
        mesh=mesh,
        in_specs=(
            P("tile", None, None),
            P("tile", None, None),
            P("member"),
            P(),
            P(),
            P(),
            P(),
            P(),
            P(),
            P(),
            P(),
        ),
        out_specs=(P("tile", "member", None), P(), P(), P()),
        check_vma=False,
    )
```

profile of v0, /device:TPU:1, one launch (start us, length us, event | category | flops | bytes accessed | tf_op | source)
XLA Modules:
  0.0 224.7 jit_solution(10726558792256080895)
XLA Ops:
  7.2 0.8 fusion.160
  8.0 4.0 %collective-permute-start = (bf16[1,32,256]{2,1,0:T(8,128)(2,1)S(1)}, bf16[1,32,256]{2,1,0:T(8,128)(2,1)S(1)}, u32[]{:S(2)}, u32[]{:S(2)}) collective-permute-start(bf16[1,32,256]{2,1,0:T(8,128)(2,1)S(1)} %get-tuple-element.66), channel_id=1, source_target_pairs={{0,1},{1,2},{2,3},{3,4},{4,5},{5,6},{6,7},{8,9},{9,10},{10,11},{11... | collective-permute-start | bytes 49160 | tf_op jit(solution)/shard_map/ppermute | solution.py:18
  11.9 1.3 collective-permute-start.1
  13.2 0.9 fusion.146
  14.3 2.1 collective-permute-done.1
  16.4 0.9 fusion.70
  17.4 1.0 fusion.82
  18.4 1.1 fusion.75
  22.0 0.4 fusion.21
  22.5 4.2 %collective-permute-start.2 = (bf16[2,1,256,128]{3,2,1,0:T(8,128)(2,1)S(1)}, bf16[2,1,256,128]{3,2,1,0:T(8,128)(2,1)S(1)}, u32[]{:S(2)}, u32[]{:S(2)}) collective-permute-start(bf16[2,1,256,128]{3,2,1,0:T(8,128)(2,1)S(1)} %get-tuple-element.64), channel_id=1, source_target_pairs={{0,1},{1,2},{2,3},{3,4},{4,5},{5,6},{6,7},{8,9},{9,10},{10,11},{11... | collective-permute-start | bytes 393224 | tf_op jit(solution)/shard_map/ppermute | solution.py:18
  26.7 1.3 collective-permute-start.3
  28.0 0.6 collective-permute-done.2
  28.6 3.8 %collective-permute-done.3 = bf16[2,1,256,128]{3,2,1,0:T(8,128)(2,1)S(1)} collective-permute-done((bf16[2,1,256,128]{3,2,1,0:T(8,128)(2,1)S(1)}, bf16[2,1,256,128]{3,2,1,0:T(8,128)(2,1)S(1)}, u32[]{:S(2)}, u32[]{:S(2)}) %collective-permute-start.3) | collective-permute-done | bytes 131104 | tf_op jit(solution)/shard_map/ppermute | solution.py:19
  35.0 0.6 fusion.29
  35.6 3.3 %collective-permute-start.4 = (bf16[2,1,256,128]{3,2,1,0:T(8,128)(2,1)S(1)}, bf16[2,1,256,128]{3,2,1,0:T(8,128)(2,1)S(1)}, u32[]{:S(2)}, u32[]{:S(2)}) collective-permute-start(bf16[2,1,256,128]{3,2,1,0:T(8,128)(2,1)S(1)} %get-tuple-element.62), channel_id=1, source_target_pairs={{0,1},{1,2},{2,3},{3,4},{4,5},{5,6},{6,7},{8,9},{9,10},{10,11},{11... | collective-permute-start | bytes 393224 | tf_op jit(solution)/shard_map/ppermute | solution.py:18
  38.8 1.3 collective-permute-start.5
  40.1 0.7 convert_element_type.66
  41.5 0.7 dynamic-slice_convert_fusion
  42.2 2.8 %collective-permute-done.5 = bf16[2,1,256,128]{3,2,1,0:T(8,128)(2,1)S(1)} collective-permute-done((bf16[2,1,256,128]{3,2,1,0:T(8,128)(2,1)S(1)}, bf16[2,1,256,128]{3,2,1,0:T(8,128)(2,1)S(1)}, u32[]{:S(2)}, u32[]{:S(2)}) %collective-permute-start.5) | collective-permute-done | bytes 131104 | tf_op jit(solution)/shard_map/ppermute | solution.py:19
  45.3 1.1 fusion.50
  48.5 0.6 copy-done.3
  49.1 0.7 add_convert_fusion
  50.3 0.8 copy.57
  51.0 7.7 %all-to-all-start = ((bf16[2,4,32,256]{3,1,0,2:T(4,128)(2,1)}), bf16[2,4,32,256]{3,1,0,2:T(4,128)(2,1)S(1)}, u32[]{:S(2)}, u32[]{:S(2)}) async-start(bf16[2,4,32,256]{3,1,0,2:T(4,128)(2,1)} %copy.57), calls=%async_computation | async-start | bytes 262144 | tf_op jit(solution)/shard_map/all_to_all | solution.py:130
  58.7 3.6 %all-to-all-done = bf16[2,4,32,256]{3,1,0,2:T(4,128)(2,1)S(1)} async-done(((bf16[2,4,32,256]{3,1,0,2:T(4,128)(2,1)}), bf16[2,4,32,256]{3,1,0,2:T(4,128)(2,1)S(1)}, u32[]{:S(2)}, u32[]{:S(2)}) %all-to-all-start) | async-done | bytes 131104 | tf_op jit(solution)/shard_map/all_to_all | solution.py:130
  62.4 0.7 broadcast.97.clone.1
  63.1 5.7 %while.21 = (s32[]{:T(128)}, f32[8,4,8,256]{3,2,1,0:T(8,128)}, f32[8,4,8,256]{3,2,1,0:T(8,128)S(1)}, s32[]{:T(128)}) while((s32[]{:T(128)}, f32[8,4,8,256]{3,2,1,0:T(8,128)}, f32[8,4,8,256]{3,2,1,0:T(8,128)S(1)}, s32[]{:T(128)}) %tuple.52), condition=%wide.region_9.10_spmd, body=%wide.region_7.9_spmd.sunk | while | flops 188418 | bytes 459321 | solution.py:78
  63.2 0.6 bitcast_dynamic-update-slice_fusion.5
  63.9 0.6 bitcast_dynamic-update-slice_fusion.5
  64.7 0.6 bitcast_dynamic-update-slice_fusion.5
  65.4 0.6 bitcast_dynamic-update-slice_fusion.5
  66.1 0.6 bitcast_dynamic-update-slice_fusion.5
  66.8 0.6 bitcast_dynamic-update-slice_fusion.5
  67.5 0.6 bitcast_dynamic-update-slice_fusion.5
  68.2 0.6 bitcast_dynamic-update-slice_fusion.5
  68.8 1.7 multiply_convert_fusion
  70.5 4.3 %all-to-all-start.1 = ((bf16[8,4,8,256]{3,2,1,0:T(8,128)(2,1)}), bf16[8,4,8,256]{3,2,1,0:T(8,128)(2,1)S(1)}, u32[]{:S(2)}, u32[]{:S(2)}) async-start(bf16[8,4,8,256]{3,2,1,0:T(8,128)(2,1)} %multiply_convert_fusion), calls=%async_computation.1 | async-start | bytes 262144 | tf_op jit(solution)/shard_map/all_to_all | solution.py:148
  74.9 0.7 broadcast.97.clone
  75.6 5.3 %while.20 = (s32[]{:T(128)}, f32[8,4,8,256]{3,2,1,0:T(8,128)}, f32[8,4,8,256]{3,2,1,0:T(8,128)S(1)}, s32[]{:T(128)}) while((s32[]{:T(128)}, f32[8,4,8,256]{3,2,1,0:T(8,128)}, f32[8,4,8,256]{3,2,1,0:T(8,128)S(1)}, s32[]{:T(128)}) %tuple.53), condition=%wide.region_5.6_spmd, body=%wide.region_3.5_spmd.sunk | while | flops 188418 | bytes 459321 | solution.py:70
  75.6 0.6 bitcast_dynamic-update-slice_fusion.4
  76.3 0.6 bitcast_dynamic-update-slice_fusion.4
  77.0 0.6 bitcast_dynamic-update-slice_fusion.4
  77.6 0.6 bitcast_dynamic-update-slice_fusion.4
  78.3 0.6 bitcast_dynamic-update-slice_fusion.4
  79.0 0.6 bitcast_dynamic-update-slice_fusion.4
  79.6 0.6 bitcast_dynamic-update-slice_fusion.4
  80.3 0.6 bitcast_dynamic-update-slice_fusion.4
  80.9 1.0 reduce_sum.68
  82.0 0.9 fusion.13
  82.9 0.3 convolution_bitcast_fusion.7
  83.2 0.3 convolution_bitcast_fusion.6
  83.6 0.3 convolution_bitcast_fusion.5
  83.9 0.3 convolution_bitcast_fusion.9
  84.6 0.3 convolution_bitcast_fusion.4
  85.0 0.3 convolution_bitcast_fusion.3
  85.3 0.5 copy-done.4
  85.9 0.3 convolution_bitcast_fusion.1
  86.3 0.5 copy-done.7
  86.8 0.3 convolution_bitcast_fusion.2
  87.2 0.9 pad_maximum_fusion.2
  88.1 0.6 copy.71
  89.1 41.6 %all-reduce.3 = (f32[128,32]{0,1:T(8,128)}, f32[32]{0:T(128)}) all-reduce(f32[128,32]{0,1:T(8,128)S(1)} %convolution_bitcast_fusion.10, f32[32]{0:T(128)S(1)} %reduce_sum.70), channel_id=1, replica_groups=mesh['member'=4,'tile'=8] {'member','tile'}, use_global_device_ids=true, to_apply=%region_11.12 | all-reduce | flops 4128 | bytes 33024 | tf_op jit(solution)/shard_map/psum | solution.py:171
  130.7 85.3 %all-reduce.6.cloned.1.call-done = f32[3,3,128,128]{3,2,1,0:T(8,128)} async-done(((f32[3,3,128,128]{3,2,1,0:T(8,128)}), f32[3,3,128,128]{3,2,1,0:T(8,128)}) %all-reduce.6.cloned.1.call-update) | async-done | bytes 589840 | tf_op jit(solution)/shard_map/psum | solution.py:171
  216.0 1.9 copy.140
  (106 shorter events, 10.0 us)
Async XLA Ops:
  7.2 7.0 %copy-start = (f32[16,256]{1,0:T(8,128)S(1)}, f32[16,256]{1,0:T(8,128)}, u32[]{:S(2)}) copy-start(f32[16,256]{1,0:T(8,128)} %param.20) | copy-start | bytes 49156
  7.2 12.3 %copy-start.10 = (bf16[3,3,32,128]{3,2,1,0:T(8,128)(2,1)S(1)}, bf16[3,3,32,128]{3,2,1,0:T(8,128)(2,1)}, u32[]{:S(2)}) copy-start(bf16[3,3,32,128]{3,2,1,0:T(8,128)(2,1)} %param.21) | copy-start | bytes 221188
  8.0 6.3 %collective-permute-start = (bf16[1,32,256]{2,1,0:T(8,128)(2,1)S(1)}, bf16[1,32,256]{2,1,0:T(8,128)(2,1)S(1)}, u32[]{:S(2)}, u32[]{:S(2)}) collective-permute-start(bf16[1,32,256]{2,1,0:T(8,128)(2,1)S(1)} %get-tuple-element.66), channel_id=1, source_target_pairs={{0,1},{1,2},{2,3},{3,4},{4,5},{5,6},{6,7},{8,9},{9,10},{10,11},{11... | collective-permute-start | bytes 49160 | tf_op jit(solution)/shard_map/ppermute | solution.py:18
  11.9 4.5 %collective-permute-start.1 = (bf16[1,32,256]{2,1,0:T(8,128)(2,1)S(1)}, bf16[1,32,256]{2,1,0:T(8,128)(2,1)S(1)}, u32[]{:S(2)}, u32[]{:S(2)}) collective-permute-start(bf16[1,32,256]{2,1,0:T(8,128)(2,1)S(1)} %get-tuple-element.67), channel_id=1, source_target_pairs={{1,0},{2,1},{3,2},{4,3},{5,4},{6,5},{7,6},{9,8},{10,9},{11,10},{12... | collective-permute-start | bytes 49160 | tf_op jit(solution)/shard_map/ppermute | solution.py:19
  19.7 0.8 copy-start.1
  22.5 10.2 %copy-start.9 = (bf16[3,3,128,128]{3,2,1,0:T(8,128)(2,1)S(1)}, bf16[3,3,128,128]{3,2,1,0:T(8,128)(2,1)}, u32[]{:S(2)}) copy-start(bf16[3,3,128,128]{3,2,1,0:T(8,128)(2,1)} %param.22) | copy-start | bytes 884740
  22.5 6.1 %collective-permute-start.2 = (bf16[2,1,256,128]{3,2,1,0:T(8,128)(2,1)S(1)}, bf16[2,1,256,128]{3,2,1,0:T(8,128)(2,1)S(1)}, u32[]{:S(2)}, u32[]{:S(2)}) collective-permute-start(bf16[2,1,256,128]{3,2,1,0:T(8,128)(2,1)S(1)} %get-tuple-element.64), channel_id=1, source_target_pairs={{0,1},{1,2},{2,3},{3,4},{4,5},{5,6},{6,7},{8,9},{9,10},{10,11},{11... | collective-permute-start | bytes 393224 | tf_op jit(solution)/shard_map/ppermute | solution.py:18
  26.7 5.7 %collective-permute-start.3 = (bf16[2,1,256,128]{3,2,1,0:T(8,128)(2,1)S(1)}, bf16[2,1,256,128]{3,2,1,0:T(8,128)(2,1)S(1)}, u32[]{:S(2)}, u32[]{:S(2)}) collective-permute-start(bf16[2,1,256,128]{3,2,1,0:T(8,128)(2,1)S(1)} %get-tuple-element.65), channel_id=1, source_target_pairs={{1,0},{2,1},{3,2},{4,3},{5,4},{6,5},{7,6},{9,8},{10,9},{11,10},{12... | collective-permute-start | bytes 393224 | tf_op jit(solution)/shard_map/ppermute | solution.py:19
  35.6 6.7 %collective-permute-start.4 = (bf16[2,1,256,128]{3,2,1,0:T(8,128)(2,1)S(1)}, bf16[2,1,256,128]{3,2,1,0:T(8,128)(2,1)S(1)}, u32[]{:S(2)}, u32[]{:S(2)}) collective-permute-start(bf16[2,1,256,128]{3,2,1,0:T(8,128)(2,1)S(1)} %get-tuple-element.62), channel_id=1, source_target_pairs={{0,1},{1,2},{2,3},{3,4},{4,5},{5,6},{6,7},{8,9},{9,10},{10,11},{11... | collective-permute-start | bytes 393224 | tf_op jit(solution)/shard_map/ppermute | solution.py:18
  38.8 6.2 %collective-permute-start.5 = (bf16[2,1,256,128]{3,2,1,0:T(8,128)(2,1)S(1)}, bf16[2,1,256,128]{3,2,1,0:T(8,128)(2,1)S(1)}, u32[]{:S(2)}, u32[]{:S(2)}) collective-permute-start(bf16[2,1,256,128]{3,2,1,0:T(8,128)(2,1)S(1)} %get-tuple-element.63), channel_id=1, source_target_pairs={{1,0},{2,1},{3,2},{4,3},{5,4},{6,5},{7,6},{9,8},{10,9},{11,10},{12... | collective-permute-start | bytes 393224 | tf_op jit(solution)/shard_map/ppermute | solution.py:19
  42.2 4.2 %copy-start.6 = (bf16[2,1,256,128]{3,2,1,0:T(8,128)(2,1)}, bf16[2,1,256,128]{3,2,1,0:T(8,128)(2,1)S(1)}, u32[]{:S(2)}) copy-start(bf16[2,1,256,128]{3,2,1,0:T(8,128)(2,1)S(1)} %collective-permute-done.4) | copy-start | bytes 393220
  45.0 1.4 copy-start.2
  45.3 1.1 copy-start.8
  48.2 0.9 copy-start.3
  49.1 0.9 copy-start.5
  49.1 0.9 copy-start.11
  49.1 0.9 copy-start.12
  51.0 11.3 %all-to-all-start = ((bf16[2,4,32,256]{3,1,0,2:T(4,128)(2,1)}), bf16[2,4,32,256]{3,1,0,2:T(4,128)(2,1)S(1)}, u32[]{:S(2)}, u32[]{:S(2)}) async-start(bf16[2,4,32,256]{3,1,0,2:T(4,128)(2,1)} %copy.57), calls=%async_computation | async-start | bytes 262144 | tf_op jit(solution)/shard_map/all_to_all | solution.py:130
  70.5 11.4 %all-to-all-start.1 = ((bf16[8,4,8,256]{3,2,1,0:T(8,128)(2,1)}), bf16[8,4,8,256]{3,2,1,0:T(8,128)(2,1)S(1)}, u32[]{:S(2)}, u32[]{:S(2)}) async-start(bf16[8,4,8,256]{3,2,1,0:T(8,128)(2,1)} %multiply_convert_fusion), calls=%async_computation.1 | async-start | bytes 262144 | tf_op jit(solution)/shard_map/all_to_all | solution.py:148
  74.9 141.1 %all-reduce.6.cloned.1.call-start = ((), (), s32[]{:S(2)}) async-start(), calls=%async_computation.2 | async-start | bytes 1179648 | tf_op jit(solution)/shard_map/psum | solution.py:171
  85.0 0.9 copy-start.4
  85.9 0.9 copy-start.7
Sparse Core Ops, SparseCore 0:
  88.2 127.7 all-reduce.5
where the time goes:
time: 226 us; the launch traced here: 225 us
  waiting for transfers between devices  98.2 us (43%)
  blocking collectives  41.6 us (18%)
  starting transfers between devices  27.3 us (12%)
  local copies, waits for them, and re-layouts  18.2 us (8%)
  matrix products  16.1 us (7%)
  between operations  15.2 us (7%)
  other arithmetic  8.16 us (4%)
    psum x1, waiting for transfers between devices, on_device(): lax.psum((conv_grad, head_grad, bias_grad), ('member', 'tile'))  85.3 us
    psum x1, blocking collectives, on_device(): lax.psum((conv_grad, head_grad, bias_grad), ('member', 'tile'))  41.6 us
    ppermute x3, starting transfers between devices, extended(): before = lax.ppermute(last, axis, up)  11.4 us
    dynamic_update_slice x16, local copies, waits for them, and re-layouts, abs_terms(): return lax.map(abs_single, probe)  9.97 us
    ppermute x3, waiting for transfers between devices, extended(): after = lax.ppermute(first, axis, down)  8.72 us
    all_to_all x1, starting transfers between devices, on_device(): lax.all_to_all(sample_prediction, 'member', split_axis=2, concat_axis=0,...  7.66 us
    dot_general x18, matrix products, feature_conv(): jnp.einsum('mrwc,cd->mrwd', wide[:, i:i + out_rows, j:j + col_count], ker...  6.59 us
    unnamed x28, local copies, waits for them, and re-layouts  4.77 us
  transfers between devices with their start and end apart: 9, of which 6 were waited for; matrix products, arithmetic and copies ran while one was open for 5% of the time, Pallas kernels for 0%

commit v1 on v0

v1 whole, which is shorter than its diff:
```python
import functools
import math

import jax
import jax.numpy as jnp
from jax import lax
from jax.experimental import pallas as pl
from jax.experimental.pallas import tpu as pltpu
from jax.sharding import PartitionSpec as P

GRID_ROWS = 2048
HALO = 3
GELU_A = math.sqrt(2.0 / math.pi)
GELU_B = 0.044715
F32 = jnp.float32
BF16 = jnp.bfloat16


def dot(a, b, ca, cb):
    return lax.dot_general(a, b, (((ca,), (cb,)), ((), ())), preferred_element_type=F32)


def gelu(x):
    t = jnp.tanh(GELU_A * (x + GELU_B * (x * x * x)))
    return 0.5 * x * (1.0 + t)


def gelu_and_slope(x):
    sq = x * x
    t = jnp.tanh(GELU_A * (x + GELU_B * (x * sq)))
    half = 0.5 * (1.0 + t)
    slope = half + (0.5 * x) * (1.0 - t * t) * (GELU_A * (1.0 + (3.0 * GELU_B) * sq))
    return x * half, slope


def sign(d):
    return jnp.where(d > 0.0, 1.0, jnp.where(d < 0.0, -1.0, 0.0))


def kernel(
    sizes,
    coarse, target, seeds, band, bank, cond, kin, kmid, kout, head, offset,
    crps, cgrad, hgrad, bgrad,
    xin, kcat, headt, s1, s2, third, slope, dpre, fc, cot, rfac, score,
    acc, rc, rx, rt, total,
    halo_send, halo_recv, fc_send, fc_recv,
    c_send, c_recv, x_send, x_recv, t_send, t_recv,
    gt_send, gt_recv, gx_send, gx_recv, gc_send, gc_recv,
):
    M, T, mm, R, V, W, C, N = sizes
    me = lax.axis_index("member")
    tile = lax.axis_index("tile")
    X = M // 2
    core = lax.rem(me, 2)
    xi = me // 2
    members = M * mm

    def remote(src, dst, ss, rs, member, tl):
        return pltpu.make_async_remote_copy(
            src_ref=src, dst_ref=dst, send_sem=ss, recv_sem=rs,
            device_id=(member, tl), device_id_type=pl.DeviceIdType.MESH,
        )

    barrier = pltpu.get_barrier_semaphore()
    for d in range(1, M):
        pl.semaphore_signal(barrier, inc=1, device_id=(lax.rem(me + d, M), tile),
                            device_id_type=pl.DeviceIdType.MESH)
    for d in range(1, T):
        pl.semaphore_signal(barrier, inc=1, device_id=(me, lax.rem(tile + d, T)),
                            device_id_type=pl.DeviceIdType.MESH)

    xin[HALO:HALO + R] = coarse[...]
    for i in range(3):
        for j in range(3):
            kcat[V * i:V * (i + 1), C * j:C * (j + 1)] = kin[3 * i + j]
    headt[...] = head[...].astype(F32).T.astype(BF16)
    noise = jnp.concatenate([bank[pl.ds(seeds[m], 1), :] for m in range(mm)], axis=0)
    latent = jnp.dot(noise, cond[...], precision=lax.Precision.HIGHEST,
                     preferred_element_type=F32)
    rows8 = rfac.shape[0]
    row = lax.broadcasted_iota(jnp.int32, (rows8, 128), 0) + (band[0] + tile * R)
    lat = math.pi * (row.astype(F32) + 0.5) / GRID_ROWS - math.pi / 2
    rfac[...] = jnp.cos(lat) / (T * R * W)
    eye = lax.broadcasted_iota(jnp.int32, (V, V), 0) == lax.broadcasted_iota(jnp.int32, (V, V), 1)
    off_col = jnp.sum(jnp.where(eye, jnp.broadcast_to(offset[...], (V, V)), 0.0), axis=1,
                      keepdims=True)
    acc[9 * C:N, :] = jnp.zeros((N - 9 * C, 128), F32)

    pl.semaphore_wait(barrier, (M - 1) + (T - 1))

    down = remote(xin.at[R:R + HALO], xin.at[0:HALO], halo_send.at[0], halo_recv.at[0],
                  me, lax.rem(tile + 1, T))
    up = remote(xin.at[HALO:2 * HALO], xin.at[HALO + R:2 * HALO + R], halo_send.at[1],
                halo_recv.at[1], me, lax.rem(tile + T - 1, T))

    @pl.when(tile < T - 1)
    def _():
        down.start()

    @pl.when(tile > 0)
    def _():
        up.start()

    @pl.when(tile > 0)
    def _():
        down.wait_recv()

    @pl.when(tile < T - 1)
    def _():
        up.wait_recv()

    @pl.when(tile == 0)
    def _():
        xin[0:HALO] = jnp.zeros((HALO, V, W), BF16)

    @pl.when(tile == T - 1)
    def _():
        xin[HALO + R:2 * HALO + R] = jnp.zeros((HALO, V, W), BF16)

    def shift_down(x):
        w = lax.broadcasted_iota(jnp.int32, x.shape, 0)
        return jnp.where(w == 0, 0.0, pltpu.roll(x, 1, 0))

    def shift_up(x):
        w = lax.broadcasted_iota(jnp.int32, x.shape, 0)
        return jnp.where(w == W - 1, 0.0, pltpu.roll(x, W - 1, 0))

    def put_shifted(dst, m, q, x):
        dst[m, q, :, 0:C] = shift_down(x).astype(BF16)
        dst[m, q, :, C:2 * C] = x.astype(BF16)
        dst[m, q, :, 2 * C:3 * C] = shift_up(x).astype(BF16)

    def inside(grow):
        return jnp.logical_and(grow >= 0, grow < T * R)

    def first_row(q, carry):
        p = dot(xin[pl.ds(q, 3)].reshape(3 * V, W), kcat[...], 0, 0)
        base = shift_down(p[:, 0:C]) + p[:, C:2 * C] + shift_up(p[:, 2 * C:3 * C])
        centred = base - jnp.mean(base, axis=-1, keepdims=True)
        spread = jnp.mean(centred * centred, axis=-1, keepdims=True)
        normed = centred * lax.rsqrt(spread + 1e-05)
        ok = inside(tile * R + q - 2)
        for m in range(mm):
            mixed = normed * (1.0 + latent[m:m + 1, 0:C]) + latent[m:m + 1, C:2 * C]
            put_shifted(s1, m, q, jnp.where(ok, gelu(mixed), 0.0))
        return carry

    lax.fori_loop(0, R + 4, first_row, 0)

    def fc_copy(m, d, slot):
        return remote(fc.at[slot], fc.at[slot], fc_send.at[m, d - 1], fc_recv.at[m, d - 1],
                      lax.rem(me + d, M), tile)

    for m in range(mm):
        def second_row(q, carry, m=m):
            h = dot(s1[m, q], kmid[0], 1, 0)
            h = h + dot(s1[m, q + 1], kmid[1], 1, 0)
            h = h + dot(s1[m, q + 2], kmid[2], 1, 0)
            put_shifted(s2, m, q, jnp.where(inside(tile * R + q - 1), gelu(h), 0.0))
            return carry

        lax.fori_loop(0, R + 2, second_row, 0)
        slot = me * mm + m

        def out_row(r, carry, m=m, slot=slot):
            h = dot(s2[m, r], kout[0], 1, 0)
            h = h + dot(s2[m, r + 1], kout[1], 1, 0)
            h = h + dot(s2[m, r + 2], kout[2], 1, 0)
            g, s = gelu_and_slope(h)
            slope[m, r] = s
            feat = (s1[m, r + 2, :, C:2 * C].astype(F32) + g).astype(BF16)
            third[m, r] = feat
            f = dot(headt[...], feat, 1, 1) + coarse[r].astype(F32) + off_col
            fc[slot, r] = f.astype(BF16)
            return carry

        lax.fori_loop(0, R, out_row, 0)
        for d in range(1, M):
            fc_copy(m, d, slot).start()

    for m in range(mm):
        for d in range(1, M):
            fc_copy(m, d, lax.rem(me + M - d, M) * mm + m).wait_recv()

    def cot_row(r, carry):
        truth = target[r].astype(F32)
        factor = rfac[pl.ds(r, 1), 0:1]
        for m in range(mm):
            f = fc[me * mm + m, r].astype(F32)
            s = jnp.zeros_like(f)
            for j in range(members):
                s = s + sign(f - fc[j, r].astype(F32))
            c = factor * (sign(f - truth) / members - s / (members * (members - 1)))
            cb = c.astype(BF16)
            cot[m, r] = cb
            back = dot(cb, headt[...], 0, 0)
            dpre[m, r] = (back * slope[m, r]).astype(BF16)
            acc[9 * C:9 * C + V, :] += dot(cb, third[m, r], 1, 0)
            acc[9 * C + V:9 * C + V + 8, 0:V] += dot(jnp.ones((8, W), BF16), cb, 1, 1)
        return carry

    lax.fori_loop(0, R, cot_row, 0)

    for i in range(3):
        g = jnp.zeros((3 * C, C), F32)
        for m in range(mm):
            g = g + dot(s2[m, i:i + R].reshape(R * W, 3 * C), dpre[m].reshape(R * W, C), 0, 0)
        acc[3 * C * i:3 * C * (i + 1), :] = g

    half, chunk, piece = N // 2, N // M, N // (M * T)
    mate = me + 1 - 2 * core
    my_half = pl.multiple_of(core * half, 8)
    other_half = pl.multiple_of((1 - core) * half, 8)
    cc = remote(acc.at[pl.ds(other_half, half)], rc, c_send, c_recv, mate, tile)
    cc.start()

    def crps_row(r, carry):
        truth = target[r].astype(F32)
        fs = [fc[j, r].astype(F32) for j in range(members)]
        near = jnp.zeros_like(truth)
        pair = jnp.zeros_like(truth)
        for i in range(members):
            near = near + jnp.abs(fs[i] - truth)
            for j in range(i + 1, members):
                pair = pair + jnp.abs(fs[i] - fs[j])
        score[r] = near / members - (2.0 * pair) / (2 * members * (members - 1))
        return carry

    lax.fori_loop(0, R, crps_row, 0)
    share = V // M
    for k in range(M):
        @pl.when(me == k)
        def _(k=k):
            crps[...] = score[:, share * k:share * (k + 1), :]

    cc.wait_recv()
    acc[pl.ds(my_half, half), :] += rc[...]

    def x_at(x):
        return pl.multiple_of(core * half + x * chunk, 8)

    xs = []
    for d in range(1, X):
        to = lax.rem(xi + d, X)
        xs.append(remote(acc.at[pl.ds(x_at(to), chunk)], rx.at[d - 1], x_send.at[d - 1],
                         x_recv.at[d - 1], to * 2 + core, tile))
    for cp in xs:
        cp.start()
    for d in range(1, X):
        xs[d - 1].wait_recv()
        acc[pl.ds(x_at(xi), chunk), :] += rx[d - 1]

    def t_at(x, t):
        return pl.multiple_of(core * half + x * chunk + t * piece, 8)

    ts = []
    for d in range(1, T):
        to = lax.rem(tile + d, T)
        ts.append(remote(acc.at[pl.ds(t_at(xi, to), piece)], rt.at[d - 1], t_send.at[d - 1],
                         t_recv.at[d - 1], me, to))
    for cp in ts:
        cp.start()
    own = acc[pl.ds(t_at(xi, tile), piece), :]
    for d in range(1, T):
        ts[d - 1].wait_recv()
        own = own + rt[d - 1]
    total[pl.ds(t_at(xi, tile), piece), :] = own

    def here(x, t):
        return total.at[pl.ds(t_at(x, t), piece)]

    def gt_copy(d, t):
        return remote(here(xi, t), here(xi, t), gt_send.at[d - 1], gt_recv.at[d - 1],
                      me, lax.rem(tile + d, T))

    def gx_copy(d, k, x, t):
        return remote(here(x, t), here(x, t), gx_send.at[d - 1, k], gx_recv.at[d - 1, k],
                      lax.rem(xi + d, X) * 2 + core, tile)

    def gc_copy(d, k, x, t, c):
        at = pl.multiple_of(c * half + x * chunk + t * piece, 8)
        ref = total.at[pl.ds(at, piece)]
        return remote(ref, ref, gc_send.at[d, k], gc_recv.at[d, k], mate, tile)

    for d in range(1, T):
        gt_copy(d, tile).start()
    for k in range(T):
        t = lax.rem(tile + T - k, T)
        if k > 0:
            gt_copy(k, t).wait_recv()
        for d in range(1, X):
            gx_copy(d, k, xi, t).start()
        gc_copy(0, k, xi, t, core).start()
    for k in range(T):
        t = lax.rem(tile + T - k, T)
        for d in range(1, X):
            x = lax.rem(xi + X - d, X)
            gx_copy(d, k, x, t).wait_recv()
            gc_copy(d, k, x, t, core).start()
    for k in range(T):
        t = lax.rem(tile + T - k, T)
        for d in range(X):
            gc_copy(d, k, lax.rem(xi + X - d, X), t, 1 - core).wait_recv()

    cgrad[...] = total[0:9 * C, :]
    hgrad[...] = total[9 * C:9 * C + V, :].T
    bgrad[...] = total[9 * C + V:9 * C + V + 1, 0:V]

    @pl.when(tile < T - 1)
    def _():
        down.wait_send()

    @pl.when(tile > 0)
    def _():
        up.wait_send()

    for m in range(mm):
        for d in range(1, M):
            fc_copy(m, d, me * mm + m).wait_send()
    cc.wait_send()
    for cp in xs + ts:
        cp.wait_send()
    for d in range(1, T):
        gt_copy(d, tile).wait_send()
    for k in range(T):
        t = lax.rem(tile + T - k, T)
        for d in range(1, X):
            gx_copy(d, k, xi, t).wait_send()
        for d in range(X):
            gc_copy(d, k, lax.rem(xi + X - d, X), t, core).wait_send()


def on_device(coarse, target, seeds, band, bank, cond, kin, kmid, kout, head, offset):
    M, T = lax.axis_size("member"), lax.axis_size("tile")
    mm = seeds.shape[0]
    R, V, W = coarse.shape
    C = kmid.shape[3]
    unit = 8 * M * T
    N = -(-(9 * C + V + 8) // unit) * unit
    X = M // 2
    sizes = (M, T, mm, R, V, W, C, N)
    vmem = pl.BlockSpec(memory_space=pltpu.VMEM)
    smem = pl.BlockSpec(memory_space=pltpu.SMEM)
    dma = pltpu.SemaphoreType.DMA
    scratch = [
        pltpu.VMEM((R + 2 * HALO, V, W), BF16),
        pltpu.VMEM((3 * V, 3 * C), BF16),
        pltpu.VMEM((V, C), BF16),
        pltpu.VMEM((mm, R + 4, W, 3 * C), BF16),
        pltpu.VMEM((mm, R + 2, W, 3 * C), BF16),
        pltpu.VMEM((mm, R, W, C), BF16),
        pltpu.VMEM((mm, R, W, C), F32),
        pltpu.VMEM((mm, R, W, C), BF16),
        pltpu.VMEM((M * mm, R, V, W), BF16),
        pltpu.VMEM((mm, R, V, W), BF16),
        pltpu.VMEM((-(-R // 8) * 8, 128), F32),
        pltpu.VMEM((R, V, W), F32),
        pltpu.VMEM((N, C), F32),
        pltpu.VMEM((N // 2, C), F32),
        pltpu.VMEM((max(X - 1, 1), N // M, C), F32),
        pltpu.VMEM((T - 1, N // (M * T), C), F32),
        pltpu.VMEM((N, C), F32),
        dma((2,)), dma((2,)), dma((mm, M - 1)), dma((mm, M - 1)),
        dma, dma, dma((max(X - 1, 1),)), dma((max(X - 1, 1),)), dma((T - 1,)), dma((T - 1,)),
        dma((T - 1,)), dma((T - 1,)), dma((max(X - 1, 1), T)), dma((max(X - 1, 1), T)),
        dma((X, T)), dma((X, T)),
    ]
    crps, cgrad, hgrad, bgrad = pl.pallas_call(
        functools.partial(kernel, sizes),
        out_shape=(
            jax.ShapeDtypeStruct((R, V // M, W), F32),
            jax.ShapeDtypeStruct((9 * C, C), F32),
            jax.ShapeDtypeStruct((C, V), F32),
            jax.ShapeDtypeStruct((1, V), F32),
        ),
        in_specs=[vmem, vmem, smem, smem] + [vmem] * 7,
        out_specs=(vmem,) * 4,
        scratch_shapes=scratch,
        compiler_params=pltpu.CompilerParams(
            collective_id=0, has_side_effects=True, vmem_limit_bytes=48 * 1024 * 1024
        ),
    )(
        coarse, target, seeds, band, bank, cond,
        kin.reshape(9, V, C), kmid.reshape(3, 3 * C, C), kout.reshape(3, 3 * C, C),
        head, offset.reshape(1, V),
    )
    return crps, cgrad.reshape(3, 3, C, C), hgrad, bgrad.reshape(V)


def solution(mesh):
    return jax.shard_map(
        on_device,
        mesh=mesh,
        in_specs=(P("tile", None, None), P("tile", None, None), P("member")) + (P(),) * 8,
        out_specs=(P("tile", "member", None), P(), P(), P()),
        check_vma=False,
    )
```

time: 226 us -> 61.7 us (0.27)
  waiting for transfers between devices: 98.2 us -> 0 us
  Pallas kernels: 0 us -> 52.1 us
  blocking collectives: 41.6 us -> 0 us
  starting transfers between devices: 27.3 us -> 0 us
  matrix products: 16.1 us -> 0 us
  between operations: 15.2 us -> 1.38 us
  local copies, waits for them, and re-layouts: 18.2 us -> 7.85 us
  other arithmetic: 8.16 us -> 0 us
    psum x1 -> x0, waiting for transfers between devices: 85.3 us -> none  [on_device(): lax.psum((conv_grad, head_grad, bias_grad), ('member', 'tile'))]
    pallas_call x0 -> x1, Pallas kernels: none -> 52.1 us  [on_device(): pl.pallas_call(functools.partial(kernel, sizes), out_shape=(jax.ShapeDtyp...]
    psum x1 -> x0, blocking collectives: 41.6 us -> none  [on_device(): lax.psum((conv_grad, head_grad, bias_grad), ('member', 'tile'))]
    dot_general x41 -> x0, matrix products: 16.1 us -> none  [the longest x18 6.59 us: feature_conv(): jnp.einsum('mrwc,cd->mrwd', wide[:, i:i + out_rows, j:j + col_count], ker...]
    ppermute x6 -> x0, starting transfers between devices: 15.3 us -> none  [the longest x3 11.4 us: extended(): before = lax.ppermute(last, axis, up)]
    all_to_all x2 -> x0, starting transfers between devices: 12 us -> none  [the longest x1 7.66 us: on_device(): lax.all_to_all(sample_prediction, 'member', split_axis=2, concat_axis=0,...]
    dynamic_update_slice x16 -> x0, local copies, waits for them, and re-layouts: 9.97 us -> none  [abs_terms(): return lax.map(abs_single, probe)]
    ppermute x6 -> x0, waiting for transfers between devices: 9.35 us -> none  [the longest x3 8.72 us: extended(): after = lax.ppermute(first, axis, down)]
  transfers between devices with their start and end apart: 9 -> 0, of which waited for: 6 -> 0; matrix products, arithmetic and copies ran while one was open for 5% -> 0% of each run, Pallas kernels for 0% -> 0%
where the time goes in v1:
time: 61.7 us; the launch traced here: 61.3 us
  Pallas kernels  52.1 us (84%)
  local copies, waits for them, and re-layouts  7.85 us (13%)
  between operations  1.38 us (2%)
    pallas_call x1, Pallas kernels, on_device(): pl.pallas_call(functools.partial(kernel, sizes), out_shape=(jax.ShapeDtyp...  52.1 us
    unnamed x22, local copies, waits for them, and re-layouts  7.85 us

profile of v1, /device:TPU:1, one launch (start us, length us, event | category | flops | bytes accessed | tf_op | source)
XLA Modules:
  0.0 61.3 jit_solution(11609732855795034631)
XLA Ops:
  0.6 0.0 copy-start.2
  1.3 0.8 %copy.15.bank = f32[64,16]{1,0:T(8,128)S(1)} copy(f32[64,16]{0,1:T(8,128)} %param.15) | data formatting | bytes 8192 | tf_op args[4]
  2.1 0.0 copy-start.5
  2.1 0.0 copy-start.6
  2.1 0.0 copy-start.7
  2.1 0.8 %copy.16.head = bf16[128,32]{1,0:T(8,128)(2,1)S(1)} copy(bf16[128,32]{0,1:T(8,128)(2,1)} %param.20) | data formatting | bytes 16384 | tf_op args[9]
  3.0 0.0 copy-done.2
  3.0 0.0 copy-done.5
  3.0 0.0 copy-done.6
  3.0 0.0 copy-done.7
  3.0 0.0 copy-start
  3.0 1.0 %copy-done = bf16[3,3,128,128]{3,2,1,0:T(8,128)(2,1)S(1)} copy-done((bf16[3,3,128,128]{3,2,1,0:T(8,128)(2,1)S(1)}, bf16[3,3,128,128]{3,2,1,0:T(8,128)(2,1)}, u32[]{:S(2)}) %copy-start) | copy-done | bytes 294936
  4.0 0.0 copy-start.1
  4.0 1.0 %copy-done.1 = bf16[3,3,128,128]{3,2,1,0:T(8,128)(2,1)S(1)} copy-done((bf16[3,3,128,128]{3,2,1,0:T(8,128)(2,1)S(1)}, bf16[3,3,128,128]{3,2,1,0:T(8,128)(2,1)}, u32[]{:S(2)}) %copy-start.1) | copy-done | bytes 294936
  4.9 0.0 copy-start.3
  4.9 0.8 %copy-done.3 = bf16[4,32,256]{2,1,0:T(8,128)(2,1)S(1)} copy-done((bf16[4,32,256]{2,1,0:T(8,128)(2,1)S(1)}, bf16[4,32,256]{2,1,0:T(8,128)(2,1)}, u32[]{:S(2)}) %copy-start.3) | copy-done | bytes 65560
  5.8 0.0 copy-start.4
  5.8 0.8 %copy-done.4 = bf16[4,32,256]{2,1,0:T(8,128)(2,1)S(1)} copy-done((bf16[4,32,256]{2,1,0:T(8,128)(2,1)S(1)}, bf16[4,32,256]{2,1,0:T(8,128)(2,1)}, u32[]{:S(2)}) %copy-start.4) | copy-done | bytes 65560
  6.6 52.1 %shard_map.138 = (f32[4,8,256]{2,1,0:T(8,128)S(1)}, f32[1152,128]{1,0:T(8,128)S(1)}, f32[128,32]{1,0:T(8,128)S(1)}, f32[1,32]{1,0:T(1,128)S(1)}) custom-call(bf16[4,32,256]{2,1,0:T(8,128)(2,1)S(1)} %copy-done.3, bf16[4,32,256]{2,1,0:T(8,128)(2,1)S(1)} %copy-done.4, s32[2]{0:T(128)S(1)} %copy-done.6, s32[1]{0:T(128)S(6)} %copy.21.band, ...), custom_call_target="tpu_custom_call" | custom-call | tf_op jit(solution)/shard_map/pallas_call | solution.py:368
  58.7 0.7 %copy.17 = f32[128,32]{0,1:T(8,128)} copy(f32[128,32]{1,0:T(8,128)S(1)} %get-tuple-element.14) | data formatting | bytes 32768
  59.4 0.6 %copy.22 = f32[4,8,256]{2,1,0:T(8,128)} copy(f32[4,8,256]{2,1,0:T(8,128)S(1)} %get-tuple-element.20) | data formatting | bytes 65536
  60.0 0.8 %copy.23 = f32[3,3,128,128]{3,2,1,0:T(8,128)} copy(f32[3,3,128,128]{3,2,1,0:T(8,128)S(1)} %bitcast.6) | data formatting | bytes 1179648
  60.8 0.5 copy.24
Async XLA Ops:
  0.6 2.3 %copy-start.2 = (bf16[3,3,32,128]{3,2,1,0:T(8,128)(2,1)S(1)}, bf16[3,3,32,128]{3,2,1,0:T(8,128)(2,1)}, u32[]{:S(2)}) copy-start(bf16[3,3,32,128]{3,2,1,0:T(8,128)(2,1)} %param.17) | copy-start | bytes 221188
  2.1 0.9 %copy-start.5 = (f32[16,256]{1,0:T(8,128)S(1)}, f32[16,256]{1,0:T(8,128)}, u32[]{:S(2)}) copy-start(f32[16,256]{1,0:T(8,128)} %cond.1) | copy-start | bytes 49156
  2.1 0.9 %copy-start.6 = (s32[2]{0:T(128)S(1)}, s32[2]{0:T(128)}, u32[]{:S(2)}) copy-start(s32[2]{0:T(128)} %seeds.1) | copy-start | bytes 28
  2.1 0.9 %copy-start.7 = (f32[32]{0:T(128)S(1)}, f32[32]{0:T(128)}, u32[]{:S(2)}) copy-start(f32[32]{0:T(128)} %param.21) | copy-start | bytes 388
  3.0 1.0 %copy-start = (bf16[3,3,128,128]{3,2,1,0:T(8,128)(2,1)S(1)}, bf16[3,3,128,128]{3,2,1,0:T(8,128)(2,1)}, u32[]{:S(2)}) copy-start(bf16[3,3,128,128]{3,2,1,0:T(8,128)(2,1)} %param.18) | copy-start | bytes 884740
  4.0 1.0 %copy-start.1 = (bf16[3,3,128,128]{3,2,1,0:T(8,128)(2,1)S(1)}, bf16[3,3,128,128]{3,2,1,0:T(8,128)(2,1)}, u32[]{:S(2)}) copy-start(bf16[3,3,128,128]{3,2,1,0:T(8,128)(2,1)} %param.19) | copy-start | bytes 884740
  4.9 0.8 %copy-start.3 = (bf16[4,32,256]{2,1,0:T(8,128)(2,1)S(1)}, bf16[4,32,256]{2,1,0:T(8,128)(2,1)}, u32[]{:S(2)}) copy-start(bf16[4,32,256]{2,1,0:T(8,128)(2,1)} %coarse.1) | copy-start | bytes 196612
  5.8 0.8 %copy-start.4 = (bf16[4,32,256]{2,1,0:T(8,128)(2,1)S(1)}, bf16[4,32,256]{2,1,0:T(8,128)(2,1)}, u32[]{:S(2)}) copy-start(bf16[4,32,256]{2,1,0:T(8,128)(2,1)} %target.1) | copy-start | bytes 196612

commit v2 on v1

--- a/solution.py
+++ b/solution.py
@@ -39,15 +39,16 @@
 
 def kernel(
     sizes,
-    coarse, target, seeds, band, bank, cond, kin, kmid, kout, head, offset,
+    seeds, band, coarse_h, kin_h, bank_h, cond_h, offset_h, head_h, kmid_h, kout_h, target_h,
     crps, cgrad, hgrad, bgrad,
-    xin, kcat, headt, s1, s2, third, slope, dpre, fc, cot, rfac, score,
-    acc, rc, rx, rt, total,
+    kin, bank, cond, offset, headt, kmid, kout, target, in_sem,
+    xin, kcat, s1, s2, third, slope, dpre, fc, cot, rfac, score,
+    acc, rc, rx, quarter, rt, total,
     halo_send, halo_recv, fc_send, fc_recv,
     c_send, c_recv, x_send, x_recv, t_send, t_recv,
     gt_send, gt_recv, gx_send, gx_recv, gc_send, gc_recv,
 ):
-    M, T, mm, R, V, W, C, N = sizes
+    M, T, mm, R, V, W, C, E, per = sizes
     me = lax.axis_index("member")
     tile = lax.axis_index("tile")
     X = M // 2
@@ -69,14 +70,27 @@
         pl.semaphore_signal(barrier, inc=1, device_id=(me, lax.rem(tile + d, T)),
                             device_id_type=pl.DeviceIdType.MESH)
 
-    xin[HALO:HALO + R] = coarse[...]
+    loads = [
+        pltpu.make_async_copy(src, dst, in_sem.at[k])
+        for k, (src, dst) in enumerate([
+            (coarse_h, xin.at[HALO:HALO + R]), (kin_h, kin), (bank_h, bank), (cond_h, cond),
+            (offset_h, offset), (head_h, headt), (kmid_h, kmid), (kout_h, kout),
+            (target_h, target),
+        ])
+    ]
+    for cp in loads:
+        cp.start()
+
+    for cp in loads[1:6]:
+        cp.wait()
     for i in range(3):
         for j in range(3):
             kcat[V * i:V * (i + 1), C * j:C * (j + 1)] = kin[3 * i + j]
-    headt[...] = head[...].astype(F32).T.astype(BF16)
-    noise = jnp.concatenate([bank[pl.ds(seeds[m], 1), :] for m in range(mm)], axis=0)
-    latent = jnp.dot(noise, cond[...], precision=lax.Precision.HIGHEST,
-                     preferred_element_type=F32)
+    lane = lax.broadcasted_iota(jnp.int32, bank.shape, 1)
+    latent = []
+    for m in range(mm):
+        noise = jnp.sum(jnp.where(lane == seeds[m], bank[...], 0.0), axis=1, keepdims=True)
+        latent.append(jnp.sum(noise * cond[...], axis=0, keepdims=True))
     rows8 = rfac.shape[0]
     row = lax.broadcasted_iota(jnp.int32, (rows8, 128), 0) + (band[0] + tile * R)
     lat = math.pi * (row.astype(F32) + 0.5) / GRID_ROWS - math.pi / 2
@@ -84,13 +98,13 @@
     eye = lax.broadcasted_iota(jnp.int32, (V, V), 0) == lax.broadcasted_iota(jnp.int32, (V, V), 1)
     off_col = jnp.sum(jnp.where(eye, jnp.broadcast_to(offset[...], (V, V)), 0.0), axis=1,
                       keepdims=True)
-    acc[9 * C:N, :] = jnp.zeros((N - 9 * C, 128), F32)
+    acc[0:E, :] = jnp.zeros((E, C), F32)
 
     pl.semaphore_wait(barrier, (M - 1) + (T - 1))
 
-    down = remote(xin.at[R:R + HALO], xin.at[0:HALO], halo_send.at[0], halo_recv.at[0],
+    down = remote(coarse_h.at[R - HALO:R], xin.at[0:HALO], halo_send.at[0], halo_recv.at[0],
                   me, lax.rem(tile + 1, T))
-    up = remote(xin.at[HALO:2 * HALO], xin.at[HALO + R:2 * HALO + R], halo_send.at[1],
+    up = remote(coarse_h.at[0:HALO], xin.at[HALO + R:2 * HALO + R], halo_send.at[1],
                 halo_recv.at[1], me, lax.rem(tile + T - 1, T))
 
     @pl.when(tile < T - 1)
@@ -100,6 +114,8 @@
     @pl.when(tile > 0)
     def _():
         up.start()
+
+    loads[0].wait()
 
     @pl.when(tile > 0)
     def _():
@@ -132,6 +148,16 @@
 
     def inside(grow):
         return jnp.logical_and(grow >= 0, grow < T * R)
+
+    def rows(count, body):
+        step = 2 if count % 2 == 0 else 1
+
+        def several(q, carry):
+            for k in range(step):
+                body(q * step + k, carry)
+            return carry
+
+        lax.fori_loop(0, count // step, several, 0)
 
     def first_row(q, carry):
         p = dot(xin[pl.ds(q, 3)].reshape(3 * V, W), kcat[...], 0, 0)
@@ -141,11 +167,13 @@
         normed = centred * lax.rsqrt(spread + 1e-05)
         ok = inside(tile * R + q - 2)
         for m in range(mm):
-            mixed = normed * (1.0 + latent[m:m + 1, 0:C]) + latent[m:m + 1, C:2 * C]
+            mixed = normed * (1.0 + latent[m][:, 0:C]) + latent[m][:, C:2 * C]
             put_shifted(s1, m, q, jnp.where(ok, gelu(mixed), 0.0))
         return carry
 
-    lax.fori_loop(0, R + 4, first_row, 0)
+    rows(R + 4, first_row)
+    loads[6].wait()
+    loads[7].wait()
 
     def fc_copy(m, d, slot):
         return remote(fc.at[slot], fc.at[slot], fc_send.at[m, d - 1], fc_recv.at[m, d - 1],
@@ -159,7 +187,7 @@
             put_shifted(s2, m, q, jnp.where(inside(tile * R + q - 1), gelu(h), 0.0))
             return carry
 
-        lax.fori_loop(0, R + 2, second_row, 0)
+        rows(R + 2, second_row)
         slot = me * mm + m
 
         def out_row(r, carry, m=m, slot=slot):
@@ -170,14 +198,15 @@
             slope[m, r] = s
             feat = (s1[m, r + 2, :, C:2 * C].astype(F32) + g).astype(BF16)
             third[m, r] = feat
-            f = dot(headt[...], feat, 1, 1) + coarse[r].astype(F32) + off_col
+            f = dot(headt[...], feat, 1, 1) + xin[HALO + r].astype(F32) + off_col
             fc[slot, r] = f.astype(BF16)
             return carry
 
-        lax.fori_loop(0, R, out_row, 0)
+        rows(R, out_row)
         for d in range(1, M):
             fc_copy(m, d, slot).start()
 
+    loads[8].wait()
     for m in range(mm):
         for d in range(1, M):
             fc_copy(m, d, lax.rem(me + M - d, M) * mm + m).wait_recv()
@@ -195,24 +224,57 @@
             cot[m, r] = cb
             back = dot(cb, headt[...], 0, 0)
             dpre[m, r] = (back * slope[m, r]).astype(BF16)
-            acc[9 * C:9 * C + V, :] += dot(cb, third[m, r], 1, 0)
-            acc[9 * C + V:9 * C + V + 8, 0:V] += dot(jnp.ones((8, W), BF16), cb, 1, 1)
+            acc[0:V, :] += dot(cb, third[m, r], 1, 0)
+            acc[V:V + 8, 0:V] += dot(jnp.ones((8, W), BF16), cb, 1, 1)
         return carry
 
-    lax.fori_loop(0, R, cot_row, 0)
-
+    rows(R, cot_row)
+
+    mate = me + 1 - 2 * core
+    sizes_b = (E, 3 * C, 3 * C, 3 * C)
+
+    def mine(b, c, x, part):
+        first = sum(sizes_b[:b]) + c * (sizes_b[b] // 2) + x * (sizes_b[b] // M)
+        return pl.ds(pl.multiple_of(first, 8), part)
+
+    def c_copy(b):
+        h = sizes_b[b] // 2
+        at = sum(sizes_b[:b]) // 2
+        return remote(acc.at[mine(b, 1 - core, 0, h)], rc.at[at:at + h], c_send.at[b],
+                      c_recv.at[b], mate, tile)
+
+    def x_copy(b, d):
+        part = sizes_b[b] // M
+        at = sum(sizes_b[:b]) // M
+        to = lax.rem(xi + d, X)
+        return remote(acc.at[mine(b, core, to, part)], rx.at[d - 1, at:at + part],
+                      x_send.at[d - 1, b], x_recv.at[d - 1, b], to * 2 + core, tile)
+
+    def core_sum(b):
+        h = sizes_b[b] // 2
+        at = sum(sizes_b[:b]) // 2
+        c_copy(b).wait_recv()
+        acc[mine(b, core, 0, h), :] += rc[at:at + h]
+        for d in range(1, X):
+            x_copy(b, d).start()
+
+    def chunk_sum(b):
+        part = sizes_b[b] // M
+        at = sum(sizes_b[:b]) // M
+        own = acc[mine(b, core, xi, part), :]
+        for d in range(1, X):
+            x_copy(b, d).wait_recv()
+            own = own + rx[d - 1, at:at + part]
+        quarter[at:at + part, :] = own
+
+    c_copy(0).start()
     for i in range(3):
         g = jnp.zeros((3 * C, C), F32)
         for m in range(mm):
             g = g + dot(s2[m, i:i + R].reshape(R * W, 3 * C), dpre[m].reshape(R * W, C), 0, 0)
-        acc[3 * C * i:3 * C * (i + 1), :] = g
-
-    half, chunk, piece = N // 2, N // M, N // (M * T)
-    mate = me + 1 - 2 * core
-    my_half = pl.multiple_of(core * half, 8)
-    other_half = pl.multiple_of((1 - core) * half, 8)
-    cc = remote(acc.at[pl.ds(other_half, half)], rc, c_send, c_recv, mate, tile)
-    cc.start()
+        acc[E + 3 * C * i:E + 3 * C * (i + 1), :] = g
+        c_copy(i + 1).start()
+        core_sum(i)
 
     def crps_row(r, carry):
         truth = target[r].astype(F32)
@@ -226,29 +288,18 @@
         score[r] = near / members - (2.0 * pair) / (2 * members * (members - 1))
         return carry
 
-    lax.fori_loop(0, R, crps_row, 0)
+    core_sum(3)
+    rows(R, crps_row)
     share = V // M
     for k in range(M):
         @pl.when(me == k)
         def _(k=k):
             crps[...] = score[:, share * k:share * (k + 1), :]
 
-    cc.wait_recv()
-    acc[pl.ds(my_half, half), :] += rc[...]
-
-    def x_at(x):
-        return pl.multiple_of(core * half + x * chunk, 8)
-
-    xs = []
-    for d in range(1, X):
-        to = lax.rem(xi + d, X)
-        xs.append(remote(acc.at[pl.ds(x_at(to), chunk)], rx.at[d - 1], x_send.at[d - 1],
-                         x_recv.at[d - 1], to * 2 + core, tile))
-    for cp in xs:
-        cp.start()
-    for d in range(1, X):
-        xs[d - 1].wait_recv()
-        acc[pl.ds(x_at(xi), chunk), :] += rx[d - 1]
+    for b in range(4):
+        chunk_sum(b)
+
+    half, chunk, piece = X * per, per, per // T
 
     def t_at(x, t):
         return pl.multiple_of(core * half + x * chunk + t * piece, 8)
@@ -256,11 +307,11 @@
     ts = []
     for d in range(1, T):
         to = lax.rem(tile + d, T)
-        ts.append(remote(acc.at[pl.ds(t_at(xi, to), piece)], rt.at[d - 1], t_send.at[d - 1],
+        ts.append(remote(quarter.at[pl.ds(pl.multiple_of(to * piece, 8), piece)], rt.at[d - 1], t_send.at[d - 1],
                          t_recv.at[d - 1], me, to))
     for cp in ts:
         cp.start()
-    own = acc[pl.ds(t_at(xi, tile), piece), :]
+    own = quarter[pl.ds(pl.multiple_of(tile * piece, 8), piece), :]
     for d in range(1, T):
         ts[d - 1].wait_recv()
         own = own + rt[d - 1]
@@ -302,9 +353,14 @@
         for d in range(X):
             gc_copy(d, k, lax.rem(xi + X - d, X), t, 1 - core).wait_recv()
 
-    cgrad[...] = total[0:9 * C, :]
-    hgrad[...] = total[9 * C:9 * C + V, :].T
-    bgrad[...] = total[9 * C + V:9 * C + V + 1, 0:V]
+    extra, part = E // M, 3 * C // M
+    for q in range(M):
+        for i in range(3):
+            at = per * q + extra + part * i
+            cgrad[3 * C * i + part * q:3 * C * i + part * (q + 1), :] = total[at:at + part, :]
+    hgrad[...] = total[0:V, :]
+    at = per * (V // extra) + V % extra
+    bgrad[...] = total[at:at + 1, 0:V]
 
     @pl.when(tile < T - 1)
     def _():
@@ -317,8 +373,11 @@
     for m in range(mm):
         for d in range(1, M):
             fc_copy(m, d, me * mm + m).wait_send()
-    cc.wait_send()
-    for cp in xs + ts:
+    for b in range(4):
+        c_copy(b).wait_send()
+        for d in range(1, X):
+            x_copy(b, d).wait_send()
+    for cp in ts:
         cp.wait_send()
     for d in range(1, T):
         gt_copy(d, tile).wait_send()
@@ -335,17 +394,28 @@
     mm = seeds.shape[0]
     R, V, W = coarse.shape
     C = kmid.shape[3]
-    unit = 8 * M * T
-    N = -(-(9 * C + V + 8) // unit) * unit
+    extra = -(-V // 8) * 8
+    while (9 * C // M + extra) % (8 * T) or extra * M < V + 8:
+        extra += 8
+    E, per = extra * M, 9 * C // M + extra
+    N = per * M
     X = M // 2
-    sizes = (M, T, mm, R, V, W, C, N)
+    sizes = (M, T, mm, R, V, W, C, E, per)
     vmem = pl.BlockSpec(memory_space=pltpu.VMEM)
     smem = pl.BlockSpec(memory_space=pltpu.SMEM)
     dma = pltpu.SemaphoreType.DMA
     scratch = [
+        pltpu.VMEM((9, V, C), BF16),
+        pltpu.VMEM(bank.shape[::-1], F32),
+        pltpu.VMEM(cond.shape, F32),
+        pltpu.VMEM((1, V), F32),
+        pltpu.VMEM((V, C), BF16),
+        pltpu.VMEM((3, 3 * C, C), BF16),
+        pltpu.VMEM((3, 3 * C, C), BF16),
+        pltpu.VMEM((R, V, W), BF16),
+        dma((9,)),
         pltpu.VMEM((R + 2 * HALO, V, W), BF16),
         pltpu.VMEM((3 * V, 3 * C), BF16),
-        pltpu.VMEM((V, C), BF16),
         pltpu.VMEM((mm, R + 4, W, 3 * C), BF16),
         pltpu.VMEM((mm, R + 2, W, 3 * C), BF16),
         pltpu.VMEM((mm, R, W, C), BF16),
@@ -357,11 +427,12 @@
         pltpu.VMEM((R, V, W), F32),
         pltpu.VMEM((N, C), F32),
         pltpu.VMEM((N // 2, C), F32),
-        pltpu.VMEM((max(X - 1, 1), N // M, C), F32),
+        pltpu.VMEM((max(X - 1, 1), per, C), F32),
+        pltpu.VMEM((per, C), F32),
         pltpu.VMEM((T - 1, N // (M * T), C), F32),
         pltpu.VMEM((N, C), F32),
         dma((2,)), dma((2,)), dma((mm, M - 1)), dma((mm, M - 1)),
-        dma, dma, dma((max(X - 1, 1),)), dma((max(X - 1, 1),)), dma((T - 1,)), dma((T - 1,)),
+        dma((4,)), dma((4,)), dma((max(X - 1, 1), 4)), dma((max(X - 1, 1), 4)), dma((T - 1,)), dma((T - 1,)),
         dma((T - 1,)), dma((T - 1,)), dma((max(X - 1, 1), T)), dma((max(X - 1, 1), T)),
         dma((X, T)), dma((X, T)),
     ]
@@ -370,21 +441,20 @@
         out_shape=(
             jax.ShapeDtypeStruct((R, V // M, W), F32),
             jax.ShapeDtypeStruct((9 * C, C), F32),
-            jax.ShapeDtypeStruct((C, V), F32),
+            jax.ShapeDtypeStruct((V, C), F32),
             jax.ShapeDtypeStruct((1, V), F32),
         ),
-        in_specs=[vmem, vmem, smem, smem] + [vmem] * 7,
+        in_specs=[smem, smem] + [pl.BlockSpec(memory_space=pltpu.HBM)] * 9,
         out_specs=(vmem,) * 4,
         scratch_shapes=scratch,
         compiler_params=pltpu.CompilerParams(
-            collective_id=0, has_side_effects=True, vmem_limit_bytes=48 * 1024 * 1024
+            collective_id=0, has_side_effects=True, vmem_limit_bytes=63 * 1024 * 1024
         ),
     )(
-        coarse, target, seeds, band, bank, cond,
-        kin.reshape(9, V, C), kmid.reshape(3, 3 * C, C), kout.reshape(3, 3 * C, C),
-        head, offset.reshape(1, V),
+        seeds, band, coarse, kin.reshape(9, V, C), bank.T, cond, offset.reshape(1, V), head.T,
+        kmid.reshape(3, 3 * C, C), kout.reshape(3, 3 * C, C), target,
     )
-    return crps, cgrad.reshape(3, 3, C, C), hgrad, bgrad.reshape(V)
+    return crps, cgrad.reshape(3, 3, C, C), hgrad.T, bgrad.reshape(V)
 
 
 def solution(mesh):

time: 61.7 us -> 55 us (0.89)
  local copies, waits for them, and re-layouts: 7.85 us -> 4.45 us
  Pallas kernels: 52.1 us -> 49 us
    unnamed x22 -> x8, local copies, waits for them, and re-layouts: 7.85 us -> 4.45 us
    pallas_call x1, Pallas kernels: 52.1 us -> 49 us  [on_device(): pl.pallas_call(functools.partial(kernel, sizes), out_shape=(jax.ShapeDtyp...]
where the time goes in v2:
time: 55 us; the launch traced here: 54.8 us
  Pallas kernels  49 us (89%)
  local copies, waits for them, and re-layouts  4.45 us (8%)
  between operations  1.29 us (2%)
    pallas_call x1, Pallas kernels, on_device(): pl.pallas_call(functools.partial(kernel, sizes), out_shape=(jax.ShapeDtyp...  49 us
    unnamed x8, local copies, waits for them, and re-layouts  4.45 us

profile of v2, /device:TPU:1, one launch (start us, length us, event | category | flops | bytes accessed | tf_op | source)
XLA Modules:
  0.0 54.8 jit_solution(8413599530267443819)
XLA Ops:
  1.3 49.0 %shard_map.138 = (f32[4,8,256]{2,1,0:T(8,128)}, f32[1152,128]{1,0:T(8,128)}, f32[32,128]{1,0:T(8,128)}, f32[1,32]{1,0:T(1,128)}) custom-call(s32[2]{0:T(128)} %seeds.1, s32[1]{0:T(128)S(6)} %copy.19.band, bf16[4,32,256]{2,1,0:T(8,128)(2,1)} %coarse_h.1, bf16[9,32,128]{2,1,0:T(8,128)(2,1)} %bitcast.12, f32[16,64]{1,0:T(8,128)} %bitcast.14, f32[16,256]{1,0:T(8,128)} %cond_h.1, ...), custom_call_target="tpu_custom_call" | custom-call | tf_op jit(solution)/shard_map/pallas_call | solution.py:439
  50.3 1.4 %copy.20 = f32[4,8,256]{2,1,0:T(8,128)} copy(f32[4,8,256]{2,1,0:T(8,128)} %get-tuple-element.16) | data formatting | bytes 65536
  51.7 0.0 copy-start
  51.7 1.9 %copy.21 = f32[3,3,128,128]{3,2,1,0:T(8,128)} copy(f32[3,3,128,128]{3,2,1,0:T(8,128)} %bitcast.9) | data formatting | bytes 1179648
  53.6 0.0 copy-done
  53.6 0.0 copy-start.1
  53.6 0.6 %copy.22 = f32[128,32]{0,1:T(8,128)} copy(f32[128,32]{0,1:T(8,128)S(1)} %bitcast.13) | data formatting | bytes 32768
  54.2 0.0 copy-done.1
  54.2 0.5 copy.23
Async XLA Ops:
  51.7 1.9 %copy-start = (f32[32,128]{1,0:T(8,128)S(1)}, f32[32,128]{1,0:T(8,128)}, u32[]{:S(2)}) copy-start(f32[32,128]{1,0:T(8,128)} %get-tuple-element.10) | copy-start | bytes 49156
  53.6 0.6 %copy-start.1 = (f32[1,32]{1,0:T(1,128)S(1)}, f32[1,32]{1,0:T(1,128)}, u32[]{:S(2)}) copy-start(f32[1,32]{1,0:T(1,128)} %get-tuple-element.11) | copy-start | bytes 388

commit v3 on v2

--- a/solution.py
+++ b/solution.py
@@ -150,7 +150,11 @@
         return jnp.logical_and(grow >= 0, grow < T * R)
 
     def rows(count, body):
-        step = 2 if count % 2 == 0 else 1
+        step = max(k for k in (1, 2, 3, 4) if count % k == 0)
+        if step == count:
+            for k in range(count):
+                body(k, 0)
+            return
 
         def several(q, carry):
             for k in range(step):
@@ -448,11 +452,11 @@
         out_specs=(vmem,) * 4,
         scratch_shapes=scratch,
         compiler_params=pltpu.CompilerParams(
-            collective_id=0, has_side_effects=True, vmem_limit_bytes=63 * 1024 * 1024
+            collective_id=0, has_side_effects=True, vmem_limit_bytes=48 * 1024 * 1024
         ),
     )(
-        seeds, band, coarse, kin.reshape(9, V, C), bank.T, cond, offset.reshape(1, V), head.T,
-        kmid.reshape(3, 3 * C, C), kout.reshape(3, 3 * C, C), target,
+        seeds, band, *(pltpu.with_memory_space_constraint(z, pltpu.HBM) for z in (coarse, kin.reshape(9, V, C), bank.T, cond, offset.reshape(1, V), head.T,
+        kmid.reshape(3, 3 * C, C), kout.reshape(3, 3 * C, C), target)),
     )
     return crps, cgrad.reshape(3, 3, C, C), hgrad.T, bgrad.reshape(V)
 

time: 55 us -> 51.3 us (0.933)
  Pallas kernels: 49 us -> 46.6 us
  local copies, waits for them, and re-layouts: 4.45 us -> 3.2 us
    pallas_call x1, Pallas kernels: 49 us -> 46.6 us  [on_device(): pl.pallas_call(functools.partial(kernel, sizes), out_shape=(jax.ShapeDtyp...]
    unnamed x8 -> x6, local copies, waits for them, and re-layouts: 4.45 us -> 3.2 us
where the time goes in v3:
time: 51.3 us; the launch traced here: 51.1 us
  Pallas kernels  46.6 us (91%)
  local copies, waits for them, and re-layouts  3.2 us (6%)
  between operations  1.3 us (3%)
    pallas_call x1, Pallas kernels, on_device(): pl.pallas_call(functools.partial(kernel, sizes), out_shape=(jax.ShapeDtyp...  46.6 us
    unnamed x6, local copies, waits for them, and re-layouts  3.2 us

profile of v3, /device:TPU:1, one launch (start us, length us, event | category | flops | bytes accessed | tf_op | source)
XLA Modules:
  0.0 51.1 jit_solution(1319225171352123558)
XLA Ops:
  1.3 0.0 copy-start
  1.3 0.6 %copy-done = s32[2]{0:T(128)S(1)} copy-done((s32[2]{0:T(128)S(1)}, s32[2]{0:T(128)}, u32[]{:S(2)}) %copy-start) | copy-done | bytes 32
  1.9 46.6 %shard_map.138 = (f32[4,8,256]{2,1,0:T(8,128)S(1)}, f32[1152,128]{1,0:T(8,128)S(1)}, f32[32,128]{1,0:T(8,128)S(1)}, f32[1,32]{1,0:T(1,128)S(1)}) custom-call(s32[2]{0:T(128)S(1)} %copy-done, s32[1]{0:T(128)S(6)} %copy.19.band, bf16[4,32,256]{2,1,0:T(8,128)(2,1)} %coarse_h.1, bf16[9,32,128]{2,1,0:T(8,128)(2,1)} %bitcast.14, f32[16,64]{1,0:T(8,128)} %bitcast.15, ...), custom_call_target="tpu_custom_call" | custom-call | tf_op jit(solution)/shard_map/pallas_call | solution.py:443
  48.6 0.6 %copy.20 = f32[4,8,256]{2,1,0:T(8,128)} copy(f32[4,8,256]{2,1,0:T(8,128)S(1)} %get-tuple-element.16) | data formatting | bytes 65536
  49.2 0.8 %copy.21 = f32[3,3,128,128]{3,2,1,0:T(8,128)} copy(f32[3,3,128,128]{3,2,1,0:T(8,128)S(1)} %bitcast.9) | data formatting | bytes 1179648
  50.0 0.6 %copy.22 = f32[128,32]{0,1:T(8,128)} copy(f32[128,32]{0,1:T(8,128)S(1)} %bitcast.10) | data formatting | bytes 32768
  50.6 0.5 %copy.23 = f32[32]{0:T(128)} copy(f32[32]{0:T(128)S(1)} %bitcast.11) | data formatting | bytes 256
Async XLA Ops:
  1.3 0.7 %copy-start = (s32[2]{0:T(128)S(1)}, s32[2]{0:T(128)}, u32[]{:S(2)}) copy-start(s32[2]{0:T(128)} %seeds.1) | copy-start | bytes 28
